TPU v7x, 256 devices: a whole 4x4x8 slice. The times are simulated.
256 devices in a mesh: freq: 8 (over z), row: 4 (over x), col: 8 (over y, core).
Axes of the slice: x: 4, y: 4, z: 8, core: 2. Of those that a mesh axis runs over, the one named last changes fastest.
Arguments:
- prior_factor: bfloat16 [8, 26624, 1024], P('freq', ('row', 'col')), may hold values from -1 to 1, as said below
- prior_seeds: int32 [8, 26624, 512], P('freq', ('row', 'col')), may hold values from 0 to 4095
- window_seeds: int32 [8, 1024, 512], P('freq'), may hold values from 0 to 4095
- spectra: float32 [8, 1024], P('freq'), may hold values from 0.25 to 1
- nugget: float32 [8, 1024], P('freq'), may hold values from 0.6 to 1.2
- decay: float32 [8], P('freq'), may hold values from 0.2 to 2
Outputs:
- velocity: float32 [512, 1024, 256], P('freq', ('row', 'col'))
Inputs may be any that keep to these rules, and one draw needn't show every extreme that they name: `prior_factor`: every entry is smaller in magnitude than 0.95 / (sqrt(26624) + sqrt(1024)), and window_matrix is positive definite.
All inputs are finite; a program needn't handle non-finite values.
Results may differ from a plain program's by a relative error of at most 0.00087.
Values sent between devices are 32-bit elements; how exact they have to be, the bound alone decides.
No kernel may reach another device: no remote copies, remote signals or barrier semaphores. Data moves between devices by JAX's collectives and lax.ppermute only.
A program may use at most 128 MiB of HBM per device.

v0:
```python
import math

import jax
import jax.numpy as jnp
from jax import lax
from jax.sharding import PartitionSpec as P

GRID = 96
NPHASE = 4096
STEPS = 256
PRIOR = 26624
FIRST_BIN = 64


cross_weight = 0.3


def window_index(positions, window, parts):
    own = window // parts
    quarter = own // 2
    device = positions // own
    within = positions % own
    return jnp.where(
        within < quarter,
        device * quarter + within,
        window // 2 + device * quarter + within - quarter,
    )


def natural_rows(gathered, parts):
    window = gathered.shape[0]
    quarter = window // (2 * parts)
    shaped = gathered.reshape(parts, 2, quarter, gathered.shape[1])
    return jnp.transpose(shaped, (1, 0, 2, 3)).reshape(window, gathered.shape[1])


def coherence(spectra, nugget, decay, row_ids):
    window = spectra.shape[0]
    col_ids = jnp.arange(window, dtype=jnp.int32)
    row_global = PRIOR + row_ids
    col_global = PRIOR + col_ids
    row_points = row_global // 3
    col_points = col_global // 3
    row_across = (row_points % GRID).astype(jnp.float32)
    row_height = (row_points // GRID).astype(jnp.float32)
    col_across = (col_points % GRID).astype(jnp.float32)
    col_height = (col_points // GRID).astype(jnp.float32)
    distance = jnp.sqrt(
        (row_across[:, None] - col_across[None, :]) ** 2
        + (row_height[:, None] - col_height[None, :]) ** 2
    )
    coupling = jnp.where(
        (row_global % 3)[:, None] == (col_global % 3)[None, :],
        jnp.float32(1.0),
        jnp.float32(cross_weight),
    )
    row_spectra = jnp.take(spectra, row_ids)
    row_nugget = jnp.take(nugget, row_ids)
    amplitude = jnp.sqrt(row_spectra[:, None] * spectra[None, :])
    diagonal = jnp.where(
        row_ids[:, None] == col_ids[None, :], row_nugget[:, None], jnp.float32(0.0)
    )
    return coupling * amplitude * jnp.exp(-decay * distance) + diagonal


def against(picked, other):
    return lax.dot_general(
        picked, other, (((0,), (0,)), ((), ())), preferred_element_type=jnp.float32
    )


def panel_factor(window_rows, own_ids, parts):
    half = window_rows.shape[1] // 2
    first_block = natural_rows(
        lax.all_gather(window_rows[:, :half], ("row", "col"), axis=0, tiled=True), parts
    )
    leading = jnp.linalg.cholesky(first_block[:half])
    lower_block = jax.scipy.linalg.solve_triangular(leading, first_block[half:].T, lower=True).T
    panel_column = jnp.concatenate([leading, lower_block], axis=0)
    own_first = jnp.take(panel_column, own_ids, axis=0)
    updated = window_rows[:, half:] - jnp.dot(
        own_first, lower_block.T, precision=lax.Precision.HIGHEST
    )
    second_block = natural_rows(lax.all_gather(updated, ("row", "col"), axis=0, tiled=True), parts)
    trailing = jnp.linalg.cholesky(second_block[half:])
    second_column = jnp.concatenate([jnp.zeros((half, half), jnp.float32), trailing], axis=0)
    own_second = jnp.take(second_column, own_ids, axis=0)
    return jnp.concatenate([own_first, own_second], axis=1)


def synthesize(pieces):
    part_re, part_im = pieces
    freq_count = part_re.shape[0]
    freq_bins = FIRST_BIN + jnp.arange(freq_count, dtype=jnp.int32)
    sample_ids = jnp.arange(STEPS, dtype=jnp.int32)
    turns = (freq_bins[:, None] * sample_ids[None, :] % STEPS).astype(jnp.float32) * (
        2.0 * math.pi / STEPS
    )
    tables = jnp.concatenate([jnp.cos(turns), jnp.sin(turns)], axis=0)
    stacked = jnp.concatenate([part_re, -part_im], axis=0)
    return jnp.einsum("gps,gt->spt", stacked, tables, precision=lax.Precision.HIGHEST)


def shards(prior_factor, prior_seeds, window_seeds, spectra, nugget, decay):
    prior_cols = prior_factor[0]
    window = prior_cols.shape[1]
    parts = lax.axis_size(("row", "col"))
    own_rows = window // parts
    offset = lax.axis_index(("row", "col")) * own_rows
    own_ids = window_index(offset + jnp.arange(own_rows, dtype=jnp.int32), window, parts)
    seed_count = prior_seeds.shape[2]
    phases = 2.0 * math.pi / NPHASE * prior_seeds[0].astype(jnp.float32)
    waves = jnp.concatenate(
        [jnp.cos(phases).astype(jnp.bfloat16), jnp.sin(phases).astype(jnp.bfloat16)], axis=1
    )
    spectra_here = spectra[0]
    nugget_here = nugget[0]
    decay_here = decay[0]
    wanted = window_index(
        jnp.arange(lax.axis_size(("row", "col")) * own_rows, dtype=jnp.int32), window, parts
    )
    picked = jnp.take(prior_cols, wanted, axis=1)
    summed_rows = lax.psum_scatter(
        jnp.concatenate([against(picked, prior_cols), against(picked, waves)], axis=1),
        ("row", "col"),
        scatter_dimension=0,
        tiled=True,
    )
    window_rows = (
        coherence(spectra_here, nugget_here, decay_here, own_ids) - summed_rows[:, :window]
    )
    prior_yield = summed_rows[:, window:]
    factor_rows = panel_factor(window_rows, own_ids, parts)
    window_phases = 2.0 * math.pi / NPHASE * window_seeds[0].astype(jnp.float32)
    window_waves = jnp.concatenate([jnp.cos(window_phases), jnp.sin(window_phases)], axis=1)
    amplitude = prior_yield + jnp.dot(factor_rows, window_waves, precision=lax.Precision.HIGHEST)
    amp_re = amplitude[:, :seed_count][None]
    amp_im = amplitude[:, seed_count:][None]
    return synthesize(
        (
            lax.all_to_all(amp_re, "freq", split_axis=2, concat_axis=0, tiled=True),
            lax.all_to_all(amp_im, "freq", split_axis=2, concat_axis=0, tiled=True),
        )
    )


def solution(mesh):
    in_specs = (
        P("freq", ("row", "col"), None),
        P("freq", ("row", "col"), None),
        P("freq", None, None),
        P("freq", None),
        P("freq", None),
        P("freq"),
    )
    out_specs = P("freq", ("row", "col"), None)
    return jax.shard_map(shards, mesh=mesh, in_specs=in_specs, out_specs=out_specs, check_vma=False)
```

profile of v0, /device:TPU:1, one launch (start us, length us, event | category | flops | bytes accessed | tf_op | source)
XLA Modules:
  0.0 543.5 jit_solution(4224875968612760271)
XLA Ops:
  6.6 3.2 copy.50
  9.8 6.9 %fusion.16 = (bf16[832,512]{1,0:T(8,128)(2,1)}, bf16[832,512]{1,0:T(8,128)(2,1)}) fusion(s32[1,832,512]{2,1,0:T(8,128)S(1)} %copy-done.8), kind=kLoop, calls=%fused_computation.51 | loop fusion | flops 1703936 | bytes 3407872 | tf_op jit(solution)/shard_map/convert_element_type | solution.py:114
  16.7 5.2 gather_fusion
  22.0 4.2 fusion.8
  28.8 4.1 pad_maximum_fusion
  32.8 9.1 %copy.67 = f32[1024,2048]{1,0:T(8,128)} copy(f32[1024,2048]{0,1:T(8,128)} %pad_maximum_fusion) | data formatting | bytes 16777216
  44.8 99.8 %reduce-scatter.4.cloned.1.call-done = f32[32,2048]{1,0:T(8,128)} async-done(((f32[1024,2048]{1,0:T(8,128)}), f32[32,2048]{1,0:T(8,128)}) %reduce-scatter.4.cloned.1.call-update) | async-done | bytes 262160 | tf_op jit(solution)/shard_map/reduce_scatter | solution.py:123
  146.9 51.0 %all-gather.3.cloned.1.call-done = f32[1024,512]{1,0:T(8,128)} async-done(((f32[32,512]{1,0:T(8,128)}), f32[1024,512]{1,0:T(8,128)}) %all-gather.3.cloned.1.call-update) | async-done | bytes 2097168 | tf_op jit(solution)/shard_map/all_gather | solution.py:75
  201.2 11.7 %cholesky.286 = f32[128,128]{1,0:T(8,128)S(1)} custom-call(f32[128,128]{1,0:T(8,128)S(1)} %cholesky.426), custom_call_target="Cholesky" | custom-call | tf_op jit(solution)/shard_map/jit(cholesky)/cholesky | solution.py:77
  212.9 9.8 %custom-call.28 = f32[1,128,128]{1,2,0:T(8,128)S(1)} custom-call(f32[1,128,128]{2,1,0:T(8,128)S(1)} %get-tuple-element.55), custom_call_target="InvertDiagBlocksLowerTriangular" | custom-call | tf_op jit(solution)/shard_map/jit(cholesky)/cholesky | solution.py:77
  225.4 11.7 %cholesky.305 = f32[128,128]{1,0:T(8,128)S(1)} custom-call(f32[128,128]{1,0:T(8,128)S(1)} %cholesky.430), custom_call_target="Cholesky" | custom-call | tf_op jit(solution)/shard_map/jit(cholesky)/cholesky | solution.py:77
  238.5 9.9 %custom-call.29 = f32[1,128,128]{1,2,0:T(8,128)S(1)} custom-call(f32[1,128,128]{2,1,0:T(8,128)S(1)} %get-tuple-element.52), custom_call_target="InvertDiagBlocksLowerTriangular" | custom-call | tf_op jit(solution)/shard_map/jit(cholesky)/cholesky | solution.py:77
  250.0 11.7 %cholesky.326 = f32[128,128]{1,0:T(8,128)S(1)} custom-call(f32[128,128]{1,0:T(8,128)S(1)} %cholesky.435), custom_call_target="Cholesky" | custom-call | tf_op jit(solution)/shard_map/jit(cholesky)/cholesky | solution.py:77
  262.5 9.8 %custom-call.30 = f32[1,128,128]{1,2,0:T(8,128)S(1)} custom-call(f32[1,128,128]{2,1,0:T(8,128)S(1)} %get-tuple-element.49), custom_call_target="InvertDiagBlocksLowerTriangular" | custom-call | tf_op jit(solution)/shard_map/jit(cholesky)/cholesky | solution.py:77
  273.7 11.9 %cholesky.343 = f32[128,128]{1,0:T(8,128)S(1)} custom-call(f32[128,128]{1,0:T(8,128)S(1)} %convolution_subtract_fusion.9), custom_call_target="Cholesky" | custom-call | tf_op jit(solution)/shard_map/jit(cholesky)/cholesky | solution.py:77
  290.1 10.5 %while.1 = (s32[]{:T(128)}, f32[512,512]{1,0:T(8,128)S(1)}, s32[4,2]{0,1:T(2,128)S(1)}, f32[4,128,128]{2,1,0:T(8,128)}, s32[]{:T(128)}) while((s32[]{:T(128)}, f32[512,512]{1,0:T(8,128)S(1)}, s32[4,2]{0,1:T(2,128)S(1)}, f32[4,128,128]{2,1,0:T(8,128)}, s32[]{:T(128)}) %tuple.46), condition=%wide.while_cond, body=%wide.while_body.sunk | while | flops 2 | bytes 132705 | solution.py:78
  300.6 40.1 %custom-call.24 = f32[4,128,128]{1,2,0:T(8,128)S(1)} custom-call(f32[4,128,128]{2,1,0:T(8,128)} %get-tuple-element.15), custom_call_target="InvertDiagBlocksLowerTriangular" | custom-call | tf_op jit(solution)/shard_map/jit(_solve_triangular)/triangular_solve | solution.py:78
  351.7 2.8 convolution_subtract_fusion.7
  354.5 9.9 %cosine_bitcast_fusion = (f32[1024,512]{1,0:T(8,128)S(1)}, f32[1024,512]{1,0:T(8,128)}) fusion(s32[1,1024,512]{2,1,0:T(8,128)} %param.13), kind=kLoop, calls=%fused_computation.14 | loop fusion | flops 1048576 | bytes 6291456 | tf_op jit(solution)/shard_map/cos | solution.py:135
  364.4 38.4 %all-gather.5.cloned.1.call-done = f32[1024,512]{1,0:T(8,128)} async-done(((f32[32,512]{1,0:T(8,128)}), f32[1024,512]{1,0:T(8,128)}) %all-gather.5.cloned.1.call-update) | async-done | bytes 2097168 | tf_op jit(solution)/shard_map/all_gather | solution.py:84
  407.8 11.7 %cholesky.358 = f32[128,128]{1,0:T(8,128)S(1)} custom-call(f32[128,128]{1,0:T(8,128)S(1)} %cholesky.439), custom_call_target="Cholesky" | custom-call | tf_op jit(solution)/shard_map/jit(cholesky)/cholesky | solution.py:85
  419.7 9.8 %custom-call.31 = f32[1,128,128]{1,2,0:T(8,128)S(1)} custom-call(f32[1,128,128]{2,1,0:T(8,128)S(1)} %get-tuple-element.45), custom_call_target="InvertDiagBlocksLowerTriangular" | custom-call | tf_op jit(solution)/shard_map/jit(cholesky)/cholesky | solution.py:85
  432.0 11.7 %cholesky.377 = f32[128,128]{1,0:T(8,128)S(1)} custom-call(f32[128,128]{1,0:T(8,128)S(1)} %cholesky.443), custom_call_target="Cholesky" | custom-call | tf_op jit(solution)/shard_map/jit(cholesky)/cholesky | solution.py:85
  445.1 9.9 %custom-call.32 = f32[1,128,128]{1,2,0:T(8,128)S(1)} custom-call(f32[1,128,128]{2,1,0:T(8,128)S(1)} %get-tuple-element.42), custom_call_target="InvertDiagBlocksLowerTriangular" | custom-call | tf_op jit(solution)/shard_map/jit(cholesky)/cholesky | solution.py:85
  456.6 11.7 %cholesky.398 = f32[128,128]{1,0:T(8,128)S(1)} custom-call(f32[128,128]{1,0:T(8,128)S(1)} %cholesky.448), custom_call_target="Cholesky" | custom-call | tf_op jit(solution)/shard_map/jit(cholesky)/cholesky | solution.py:85
  469.0 9.8 %custom-call.33 = f32[1,128,128]{1,2,0:T(8,128)S(1)} custom-call(f32[1,128,128]{2,1,0:T(8,128)S(1)} %get-tuple-element.39), custom_call_target="InvertDiagBlocksLowerTriangular" | custom-call | tf_op jit(solution)/shard_map/jit(cholesky)/cholesky | solution.py:85
  480.3 11.7 %cholesky.415 = f32[128,128]{1,0:T(8,128)S(1)} custom-call(f32[128,128]{1,0:T(8,128)S(1)} %convolution_subtract_fusion.8), custom_call_target="Cholesky" | custom-call | tf_op jit(solution)/shard_map/jit(cholesky)/cholesky | solution.py:85
  499.6 4.1 fusion.10
  506.4 6.7 %all-to-all-start.1 = ((f32[8,1,2048]{2,1,0:T(1,128)}), f32[8,1,2048]{2,1,0:T(1,128)S(1)}, u32[]{:S(2)}, u32[]{:S(2)}) async-start(f32[8,1,2048]{2,1,0:T(1,128)} %reshape.341), calls=%async_computation.1 | async-start | bytes 131072 | tf_op jit(solution)/shard_map/all_to_all | solution.py:142
  515.4 5.0 all-to-all-done.1
  520.4 3.3 all-to-all-start
  525.3 5.7 %all-to-all-done = f32[8,1,2048]{2,1,0:T(1,128)S(1)} async-done(((f32[8,1,2048]{2,1,0:T(1,128)}), f32[8,1,2048]{2,1,0:T(1,128)S(1)}, u32[]{:S(2)}, u32[]{:S(2)}) %all-to-all-start) | async-done | bytes 65568 | tf_op jit(solution)/shard_map/all_to_all | solution.py:141
  (157 shorter events, 71.2 us)
Async XLA Ops:
  6.5 36.8 %copy-start = (f32[1,1024]{1,0:T(1,128)S(1)}, f32[1,1024]{1,0:T(1,128)}, u32[]{:S(2)}) copy-start(f32[1,1024]{1,0:T(1,128)} %param.15) | copy-start | bytes 12292
  6.5 3.2 copy-start.8
  6.5 138.0 %reduce-scatter.4.cloned.1.call-start = ((), (), s32[]{:S(2)}) async-start(), calls=%async_computation.5 | async-start | bytes 8650752 | tf_op jit(solution)/shard_map/reduce_scatter | solution.py:123
  16.7 5.3 copy-start.7
  21.9 4.2 copy-start.9
  21.9 4.2 copy-start.15
  21.9 4.2 copy-start.16
  42.0 0.7 copy-start.2
  42.0 155.9 %all-gather.3.cloned.1.call-start = ((), (), s32[]{:S(2)}) async-start(), calls=%async_computation.3 | async-start | bytes 2162688 | tf_op jit(solution)/shard_map/all_gather | solution.py:75
  146.4 256.4 %all-gather.5.cloned.1.call-start = ((), (), s32[]{:S(2)}) async-start(), calls=%async_computation.4 | async-start | bytes 2162688 | tf_op jit(solution)/shard_map/all_gather | solution.py:84
  200.2 1.0 copy-start.4
  340.7 0.8 copy-start.17
  344.9 0.7 copy-start.6
  346.9 3.8 copy-start.3
  348.1 2.1 copy-start.10
  348.2 1.9 copy-start.12
  348.4 1.8 copy-start.13
  350.0 0.7 copy-start.14
  350.7 1.0 copy-start.11
  406.8 1.0 copy-start.5
  495.7 3.9 copy-start.18
  506.4 14.0 %all-to-all-start.1 = ((f32[8,1,2048]{2,1,0:T(1,128)}), f32[8,1,2048]{2,1,0:T(1,128)S(1)}, u32[]{:S(2)}, u32[]{:S(2)}) async-start(f32[8,1,2048]{2,1,0:T(1,128)} %reshape.341), calls=%async_computation.1 | async-start | bytes 131072 | tf_op jit(solution)/shard_map/all_to_all | solution.py:142
  520.4 10.6 %all-to-all-start = ((f32[8,1,2048]{2,1,0:T(1,128)}), f32[8,1,2048]{2,1,0:T(1,128)S(1)}, u32[]{:S(2)}, u32[]{:S(2)}) async-start(f32[8,1,2048]{2,1,0:T(1,128)} %reshape.343), calls=%async_computation | async-start | bytes 131072 | tf_op jit(solution)/shard_map/all_to_all | solution.py:141
  532.3 4.4 copy-start.1
Sparse Core Ops, SparseCore 0:
  42.1 102.4 reduce-scatter.3
  147.5 50.3 all-gather.2
  354.6 48.1 all-gather.4
where the time goes:
time: 552 us; the launch traced here: 544 us
  other arithmetic  229 us (41%)
  waiting for transfers between devices  200 us (36%)
  local copies, waits for them, and re-layouts  51.2 us (9%)
  matrix products  33.1 us (6%)
  between operations  19.8 us (4%)
  starting transfers between devices  10.6 us (2%)
    reduce_scatter x1, waiting for transfers between devices, shards(): lax.psum_scatter(jnp.concatenate([against(picked, prior_cols), against(pi...  99.8 us
    another operation x15, other arithmetic, panel_factor(): leading = jnp.linalg.cholesky(first_block[:half])  79.4 us
    another operation x15, other arithmetic, panel_factor(): trailing = jnp.linalg.cholesky(second_block[half:])  79.3 us
    all_gather x1, waiting for transfers between devices, panel_factor(): lax.all_gather(window_rows[:, :half], ('row', 'col'), axis=0, tiled=True)  51 us
    another operation x3, other arithmetic, panel_factor(): jax.scipy.linalg.solve_triangular(leading, first_block[half:].T, lower=True)  41.4 us
    all_gather x1, waiting for transfers between devices, panel_factor(): lax.all_gather(updated, ('row', 'col'), axis=0, tiled=True)  38.4 us
    unnamed x45, local copies, waits for them, and re-layouts  19.2 us
  transfers between devices with their start and end apart: 5, of which 5 were waited for; matrix products, arithmetic and copies ran while one was open for 3% of the time, Pallas kernels for 0%

commit v1 on v0

v1 whole, which is shorter than its diff:
```python
import math

import jax
import jax.numpy as jnp
import numpy as np
from jax import lax
from jax.experimental import pallas as pl
from jax.experimental.pallas import tpu as pltpu
from jax.sharding import Mesh, PartitionSpec as P

GRID = 96
NPHASE = 4096
STEPS = 256
PRIOR = 26624
FIRST_BIN = 64
WINDOW = 1024
HALF = 512
SEEDS = 512
FREQS = 8
BLK = 128
CHIPS = 16
VMEM_BYTES = 40 * 1024 * 1024
EXACT = lax.Precision.HIGHEST

cross_weight = 0.3

FIRST = [(i, j) for j in range(4) for i in range(j + 1)]
SECOND = [(i, j) for j in range(4, 8) for i in range(j + 1)]
FIRST_ROWS = len(FIRST) * BLK // (2 * CHIPS)
SECOND_ROWS = len(SECOND) * BLK // (2 * CHIPS)
CHUNK = FIRST_ROWS + SECOND_ROWS

SINE = [(-1.0) ** i / math.factorial(2 * i + 1) for i in range(7)]


def params():
    return pltpu.CompilerParams(vmem_limit_bytes=VMEM_BYTES)


def pieces(local_block, rows):
    found = []
    at = 0
    while at < BLK:
        flat = local_block * BLK + at
        chip, inside = flat // rows, flat % rows
        length = min(rows - inside, BLK - at)
        found.append((at, chip, inside, length))
        at += length
    return found


def placed(blocks):
    half = len(blocks) // 2
    return [(pair, index // half, index % half) for index, pair in enumerate(blocks)]


def cosine(index):
    folded = jnp.abs(index - NPHASE // 2) - NPHASE // 4
    x = folded.astype(jnp.float32) * jnp.float32(2.0 * math.pi / NPHASE)
    y = x * x
    poly = jnp.full_like(x, SINE[-1])
    for c in SINE[-2::-1]:
        poly = poly * y + jnp.float32(c)
    return poly * x


def quarter_back(index):
    return (index + 3 * NPHASE // 4) & (NPHASE - 1)


def dot_t(a, b, precision=None):
    return lax.dot_general(a, b, (((0,), (0,)), ((), ())), preferred_element_type=jnp.float32, precision=precision)


def dot(a, b, precision=None):
    return jnp.dot(a, b, preferred_element_type=jnp.float32, precision=precision)


def schur_kernel(where_ref, cols_ref, keep_ref, send_ref):
    core = where_ref[0]
    spot = {}
    for offset, rows, blocks in ((0, FIRST_ROWS, FIRST), (FIRST_ROWS, SECOND_ROWS, SECOND)):
        for pair, half, local in placed(blocks):
            spot[pair] = (half, [(a, c, offset + i, n) for a, c, i, n in pieces(local, rows)])
    for i in range(8):
        product = dot_t(cols_ref[:, BLK * i : BLK * (i + 1)], cols_ref[:, BLK * i :])
        for j in range(i, 8):
            half, runs = spot[(i, j)]
            block = product[:, BLK * (j - i) : BLK * (j - i + 1)]

            @pl.when(core == half)
            def _():
                for at, chip, row, length in runs:
                    keep_ref[chip, row : row + length, :] = block[at : at + length, :]

            @pl.when(core != half)
            def _():
                for at, chip, row, length in runs:
                    send_ref[chip, row : row + length, :] = block[at : at + length, :]


def prior_kernel(cols_ref, seeds_ref, out_ref, waves_ref):
    for piece in range(SEEDS // BLK):
        lanes = slice(BLK * piece, BLK * (piece + 1))
        index = seeds_ref[:, lanes]
        waves_ref[:, lanes] = cosine(index).astype(jnp.bfloat16)
        waves_ref[:, SEEDS + BLK * piece : SEEDS + BLK * (piece + 1)] = cosine(quarter_back(index)).astype(jnp.bfloat16)
    for i in range(8):
        product = dot_t(cols_ref[:, BLK * i : BLK * (i + 1)], waves_ref[...])
        for part in range(8):
            owner = (8 * i + part) % 32
            row = 32 * owner + 16 * (i // 4)
            out_ref[row : row + 16, :] = product[16 * part : 16 * (part + 1), :]


def window_waves_kernel(seeds_ref, high_ref, low_ref):
    for piece in range(8):
        rows = slice(64 * piece, 64 * (piece + 1))
        lower = slice(SEEDS + 64 * piece, SEEDS + 64 * (piece + 1))
        index = seeds_ref[rows, :]
        for place, value in ((rows, cosine(index)), (lower, cosine(quarter_back(index)))):
            high = value.astype(jnp.bfloat16)
            high_ref[place, :] = high
            low_ref[place, :] = (value - high.astype(jnp.float32)).astype(jnp.bfloat16)


def bl(x, lane):
    return jnp.broadcast_to(x[:, lane : lane + 1], (8, BLK))


def bs(x, row):
    return jnp.broadcast_to(x[row : row + 1, :], (8, BLK))


def inverse_factor(rows):
    lane = lax.broadcasted_iota(jnp.int32, (8, BLK), 1)
    sub = lax.broadcasted_iota(jnp.int32, (8, BLK), 0)
    rows = list(rows)
    out = []
    for p in range(16):
        base = 8 * p
        inside = (lane >= base) & (lane < base + 8)
        here = rows[p]
        cols = [bl(here, base + k) for k in range(8)]
        a = [[bs(cols[k], i) if k >= i else None for k in range(8)] for i in range(8)]
        scale = []
        for j in range(8):
            s = lax.rsqrt(a[j][j])
            scale.append(s)
            for k in range(j + 1, 8):
                a[j][k] = a[j][k] * s
            for i in range(j + 1, 8):
                for k in range(i, 8):
                    a[i][k] = a[i][k] - a[j][i] * a[j][k]

        def forward(r):
            r = list(r)
            for j in range(8):
                r[j] = r[j] * scale[j]
                for i in range(j + 1, 8):
                    r[i] = r[i] - a[j][i] * r[j]
            return r

        eye = jnp.where(lane - base == sub, 1.0, 0.0)
        mixed = jnp.where(inside, eye, here)
        u = forward([bs(mixed, i) for i in range(8)])
        done = u[0]
        for j in range(1, 8):
            done = jnp.where(sub == j, u[j], done)
        out.append(jnp.where(lane < base + 8, done, 0.0))
        if p == 15:
            break
        n = forward([bl(rows[p + 1], base + j) for j in range(8)])
        t = [n[j] * u[j] for j in range(8)]
        t = (((t[0] + t[1]) + (t[2] + t[3])) + ((t[4] + t[5]) + t[6])) + t[7]
        rows[p + 1] = jnp.where(inside, 0.0, rows[p + 1]) - t
        if p == 14:
            continue
        w = [None] * 8
        for j in range(7, -1, -1):
            v = u[j]
            for k in range(j + 1, 8):
                v = v - a[j][k] * w[k]
            w[j] = v * scale[j]
        for r in range(p + 2, 16):
            v = jnp.where(inside, 0.0, rows[r])
            for j in range(8):
                v = v - bl(rows[r], base + j) * w[j]
            rows[r] = v
    return out


def factor_half(work_ref, upper_ref, inverse_ref, inverse_at):
    above = lax.broadcasted_iota(jnp.int32, (BLK, BLK), 0) <= lax.broadcasted_iota(jnp.int32, (BLK, BLK), 1)
    for k in range(4):
        top = BLK * k
        found = inverse_factor([work_ref[top + 8 * r : top + 8 * (r + 1), top : top + BLK] for r in range(16)])
        for r in range(16):
            inverse_ref[inverse_at + k, 8 * r : 8 * (r + 1), :] = found[r]
        row = dot(inverse_ref[inverse_at + k], work_ref[top : top + BLK, top:], EXACT)
        if k:
            upper_ref[top : top + BLK, :top] = jnp.zeros((BLK, top), jnp.float32)
        upper_ref[top : top + BLK, top : top + BLK] = jnp.where(above, row[:, :BLK], 0.0)
        if k < 3:
            upper_ref[top : top + BLK, top + BLK :] = row[:, BLK:]
        for i in range(k + 1, 4):
            work_ref[BLK * i : BLK * (i + 1), BLK * i :] -= dot_t(
                row[:, BLK * (i - k) : BLK * (i - k + 1)], row[:, BLK * (i - k) :], EXACT
            )


def unpack(core, own_ref, other_ref, blocks, rows, store):
    for pair, half, local in placed(blocks):
        for at, chip, inside, length in pieces(local, rows):
            span = slice(inside, inside + length)
            store(pair, at, length, jnp.where(core == half, own_ref[chip, span, :], other_ref[chip, span, :]))


def leading_kernel(where_ref, own_ref, other_ref, upper_ref, inverse_ref, work_ref):
    def store(pair, at, length, value):
        i, j = pair
        work_ref[BLK * i + at : BLK * i + at + length, BLK * j : BLK * (j + 1)] = value

    unpack(where_ref[0], own_ref, other_ref, FIRST, FIRST_ROWS, store)
    factor_half(work_ref, upper_ref, inverse_ref, 0)


def trailing_kernel(
    where_ref, own_ref, other_ref, upper_ref, inverse_ref, cross_ref, trailing_ref, side_ref, work_ref, spare_ref
):
    def store(pair, at, length, value):
        i, j = pair
        target, row = (side_ref, BLK * i) if i < 4 else (work_ref, BLK * (i - 4))
        target[row + at : row + at + length, BLK * (j - 4) : BLK * (j - 3)] = value

    unpack(where_ref[0], own_ref, other_ref, SECOND, SECOND_ROWS, store)
    for k in range(4):
        rows = slice(BLK * k, BLK * (k + 1))
        solved = dot(inverse_ref[k], side_ref[rows, :], EXACT)
        cross_ref[rows, :] = solved
        if k < 3:
            side_ref[BLK * (k + 1) :, :] -= dot_t(upper_ref[rows, BLK * (k + 1) :], solved, EXACT)
    for i in range(4):
        work_ref[BLK * i : BLK * (i + 1), BLK * i :] -= dot_t(
            cross_ref[:, BLK * i : BLK * (i + 1)], cross_ref[:, BLK * i :], EXACT
        )
    factor_half(work_ref, trailing_ref, spare_ref, 0)


def split(x):
    high = x.astype(jnp.bfloat16)
    return high, (x - high.astype(jnp.float32)).astype(jnp.bfloat16)


def amplitude_kernel(where_ref, upper_ref, cross_ref, trailing_ref, high_ref, low_ref, prior_ref, out_ref):
    owner = where_ref[1]
    start = pl.multiple_of(owner // 8 * BLK, BLK)
    shift = owner % 8 * 16
    column = lax.broadcasted_iota(jnp.int32, (BLK, BLK), 0)
    wanted = lax.broadcasted_iota(jnp.int32, (BLK, BLK), 1) % 32
    pick_first = jnp.where((wanted < 16) & (column == shift + wanted), 1.0, 0.0).astype(jnp.bfloat16)
    pick_second = jnp.where((wanted >= 16) & (column == shift + wanted - 16), 1.0, 0.0).astype(jnp.bfloat16)
    place = pl.ds(start, BLK)
    upper, cross, trailing = (split(r[:, place]) for r in (upper_ref, cross_ref, trailing_ref))
    mine = [
        jnp.concatenate(
            [
                (dot(upper[part], pick_first) + dot(cross[part], pick_second)).astype(jnp.bfloat16),
                dot(trailing[part], pick_second).astype(jnp.bfloat16),
            ],
            axis=0,
        )
        for part in range(2)
    ]
    repeat = jnp.where(
        lax.broadcasted_iota(jnp.int32, (32, BLK), 1) % 32 == lax.broadcasted_iota(jnp.int32, (32, BLK), 0), 1.0, 0.0
    )
    both = jnp.concatenate(mine, axis=1)
    group = lax.broadcasted_iota(jnp.int32, (16, BLK), 1) // 32
    for piece in range(8):
        rows = slice(BLK * piece, BLK * (piece + 1))
        wide = dot(high_ref[rows, :], both)
        amp = wide[:, :BLK] + wide[:, BLK:] + dot(low_ref[rows, :], mine[0])
        amp = amp + dot_t(prior_ref[:, rows], repeat, EXACT)
        for part in range(2):
            freq = 2 * (piece % 4) + part
            run = amp[64 * part : 64 * (part + 1), :]
            merged = run[:16]
            for s in range(1, 4):
                merged = jnp.where(group == s, run[16 * s : 16 * (s + 1)], merged)
            row = 16 * (piece // 4)
            out_ref[freq, row : row + 16, :] = merged


def synthesis_kernel(amp_ref, table_ref, out_ref):
    for s in range(16):
        lines = jnp.concatenate([amp_ref[:, s, :], amp_ref[:, 16 + s, :]], axis=0)
        series = dot_t(lines, table_ref[...], EXACT)
        for part in range(4):
            out_ref[16 * part + s] = series[32 * part : 32 * (part + 1), :]


SMEM = pl.BlockSpec(memory_space=pltpu.SMEM)
VMEM = pl.BlockSpec(memory_space=pltpu.VMEM)


def call(kernel, name, outs, ins, scratch=(), flops=0, moved=0):
    return pl.pallas_call(
        kernel,
        out_shape=outs,
        in_specs=ins,
        out_specs=jax.tree.map(lambda _: VMEM, outs),
        scratch_shapes=list(scratch),
        compiler_params=params(),
        cost_estimate=pl.CostEstimate(flops=flops, bytes_accessed=moved, transcendentals=0),
        name=name,
    )


def f32(*shape):
    return jax.ShapeDtypeStruct(shape, jnp.float32)


def lookup(table, index):
    result = jnp.zeros_like(index)
    for at, value in enumerate(table):
        result = jnp.where(index == at, value, result)
    return result


def coherence_chunk(spectra, nugget, decay, core, chip):
    rows, block_cols = [], []
    for count, blocks in ((FIRST_ROWS, FIRST), (SECOND_ROWS, SECOND)):
        flat = (core * CHIPS + chip) * count + jnp.arange(count, dtype=jnp.int32)
        block = flat // BLK
        rows.append(lookup([i for i, _ in blocks], block) * BLK + flat % BLK)
        block_cols.append(lookup([j for _, j in blocks], block))
    row_ids = jnp.concatenate(rows)
    block_col = jnp.concatenate(block_cols)
    col_ids = block_col[:, None] * BLK + jnp.arange(BLK, dtype=jnp.int32)[None, :]
    chosen = row_ids[:, None] == jnp.arange(WINDOW, dtype=jnp.int32)[None, :]
    row_spectra = jnp.sum(jnp.where(chosen, spectra[None, :], 0.0), axis=1)
    row_nugget = jnp.sum(jnp.where(chosen, nugget[None, :], 0.0), axis=1)
    by_block = spectra.reshape(8, BLK)
    col_spectra = jnp.zeros((CHUNK, BLK), jnp.float32)
    for j in range(8):
        col_spectra = jnp.where((block_col == j)[:, None], by_block[j][None, :], col_spectra)
    row_global = (PRIOR + row_ids)[:, None]
    col_global = PRIOR + col_ids
    row_points = row_global // 3
    col_points = col_global // 3
    across = (row_points % GRID - col_points % GRID).astype(jnp.float32)
    height = (row_points // GRID - col_points // GRID).astype(jnp.float32)
    distance = jnp.sqrt(across * across + height * height)
    coupling = jnp.where(row_global % 3 == col_global % 3, jnp.float32(1.0), jnp.float32(cross_weight))
    amplitude = jnp.sqrt(row_spectra[:, None] * col_spectra)
    diagonal = jnp.where(row_ids[:, None] == col_ids, row_nugget[:, None], jnp.float32(0.0))
    return coupling * amplitude * jnp.exp(-decay * distance) + diagonal


def tables():
    bins = FIRST_BIN + np.arange(FREQS)
    turns = (bins[:, None] * np.arange(STEPS)[None, :] % STEPS) * (2.0 * math.pi / STEPS)
    return jnp.asarray(np.concatenate([np.cos(turns), -np.sin(turns)], axis=0), jnp.float32)


CHIP_AXES = ("row", "y")


def exchange(x):
    return lax.all_to_all(x, CHIP_AXES, split_axis=0, concat_axis=0, tiled=True)


def swap(x):
    return lax.ppermute(x, "core", [(0, 1), (1, 0)])


def shards(prior_factor, prior_seeds, window_seeds, spectra, nugget, decay):
    cols = prior_factor[0]
    depth = cols.shape[0]
    core = lax.axis_index("core")
    chip = lax.axis_index(CHIP_AXES)
    owner = lax.axis_index(("row", "y", "core"))
    where = jnp.stack([core, owner]).astype(jnp.int32)

    with jax.named_scope("schur"):
        keep, send = call(
            schur_kernel, "schur", (f32(CHIPS, CHUNK, BLK),) * 2, [SMEM, VMEM], flops=10**9, moved=4 * 2**20
        )(where, cols)
        received = swap(send)
    with jax.named_scope("prior"):
        yields = call(
            prior_kernel,
            "prior",
            f32(WINDOW, 2 * SEEDS),
            [VMEM, VMEM],
            [pltpu.VMEM((depth, 2 * SEEDS), jnp.bfloat16)],
            flops=2 * 10**9,
            moved=8 * 2**20,
        )(cols, prior_seeds[0])
        prior = lax.psum_scatter(yields, ("row", "y", "core"), scatter_dimension=0, tiled=True)
    with jax.named_scope("reduce"):
        parts = exchange(keep + received)
        high, low = call(
            window_waves_kernel,
            "window_waves",
            (jax.ShapeDtypeStruct((2 * SEEDS, WINDOW), jnp.bfloat16),) * 2,
            [VMEM],
            flops=10**9,
            moved=6 * 2**20,
        )(window_seeds[0].T)
        known = coherence_chunk(spectra[0], nugget[0], decay[0], core, chip)
        chunk = known - jnp.sum(parts, axis=0)
    with jax.named_scope("gather_first"):
        own = exchange(jnp.broadcast_to(chunk[None, :FIRST_ROWS], (CHIPS, FIRST_ROWS, BLK)))
        other = swap(own)
    with jax.named_scope("gather_second"):
        rest, other = lax.optimization_barrier(
            (jnp.broadcast_to(chunk[None, FIRST_ROWS:], (CHIPS, SECOND_ROWS, BLK)), other)
        )
        own_rest = exchange(rest)
    with jax.named_scope("leading"):
        upper, inverse = call(
            leading_kernel,
            "leading",
            (f32(HALF, HALF), f32(4, BLK, BLK)),
            [SMEM, VMEM, VMEM],
            [pltpu.VMEM((HALF, HALF), jnp.float32)],
            flops=20 * 10**9,
            moved=2 * 2**20,
        )(where, own, other)
    with jax.named_scope("trailing"):
        other_rest = swap(own_rest)
        cross, trailing = call(
            trailing_kernel,
            "trailing",
            (f32(HALF, HALF), f32(HALF, HALF)),
            [SMEM, VMEM, VMEM, VMEM, VMEM],
            [pltpu.VMEM((HALF, HALF), jnp.float32)] * 2 + [pltpu.VMEM((4, BLK, BLK), jnp.float32)],
            flops=25 * 10**9,
            moved=4 * 2**20,
        )(where, own_rest, other_rest, upper, inverse)
    with jax.named_scope("amplitude"):
        amp = call(
            amplitude_kernel,
            "amplitude",
            f32(FREQS, 32, BLK),
            [SMEM] + [VMEM] * 6,
            flops=10**9,
            moved=8 * 2**20,
        )(where, upper, cross, trailing, high, low, prior)
        amp = lax.all_to_all(amp, "freq", split_axis=0, concat_axis=0, tiled=True)
    with jax.named_scope("synthesis"):
        return call(synthesis_kernel, "synthesis", f32(64, 32, STEPS), [VMEM, VMEM], flops=10**8, moved=2 * 2**20)(
            amp, tables()
        )


def solution(mesh):
    chips = Mesh(mesh.devices.reshape(8, 4, 4, 2), ("freq", "row", "y", "core"))
    own = ("row", "y", "core")
    in_specs = (
        P("freq", own, None),
        P("freq", own, None),
        P("freq", None, None),
        P("freq", None),
        P("freq", None),
        P("freq"),
    )
    return jax.shard_map(shards, mesh=chips, in_specs=in_specs, out_specs=P("freq", own, None), check_vma=False)
```

time: 552 us -> 186 us (0.34)
  other arithmetic: 229 us -> 2.3 us
  waiting for transfers between devices: 200 us -> 28.6 us
  Pallas kernels: 0 us -> 64.1 us
  local copies, waits for them, and re-layouts: 51.2 us -> 17.7 us
  matrix products: 33.1 us -> 0 us
  blocking collectives: 0 us -> 27.2 us
  starting transfers between devices: 10.6 us -> 28.5 us
    another operation x33 -> x1, other arithmetic: 200 us -> 0.07 us  [shards(): where = jnp.stack([core, owner]).astype(jnp.int32)]
    reduce_scatter x1, waiting for transfers between devices: 99.8 us -> 0.01 us  [shards(): lax.psum_scatter(yields, ('row', 'y', 'core'), scatter_dimension=0, tiled...]
    all_gather x2 -> x0, waiting for transfers between devices: 89.4 us -> none  [the longest x1 51 us: panel_factor(): lax.all_gather(window_rows[:, :half], ('row', 'col'), axis=0, tiled=True)]
    pallas_call x0 -> x7, Pallas kernels: none -> 64.1 us  [the longest x1 25.2 us: shards(): call(trailing_kernel, 'trailing', (f32(HALF, HALF), f32(HALF, HALF)), [SM...]
    all_to_all x0 -> x2, blocking collectives: none -> 27.2 us  [the longest x1 16.2 us: shards(): amp = lax.all_to_all(amp, 'freq', split_axis=0, concat_axis=0, tiled=True)]
    another operation x19 -> x0, matrix products: 17.7 us -> none  [the longest x7 6.75 us: panel_factor(): jax.scipy.linalg.solve_triangular(leading, first_block[half:].T, lower=True)]
    all_to_all x2, waiting for transfers between devices: 10.7 us -> 27.3 us  [exchange(): return lax.all_to_all(x, CHIP_AXES, split_axis=0, concat_axis=0, tiled=True)]
    dot_general x5 -> x0, matrix products: 15.5 us -> none  [the longest x2 6.78 us: against(): lax.dot_general(picked, other, (((0,), (0,)), ((), ())), preferred_elemen...]
  transfers between devices with their start and end apart: 5 -> 6, of which waited for: 5 -> 3; matrix products, arithmetic and copies ran while one was open for 3% -> 3% of each run, Pallas kernels for 0% -> 30%
where the time goes in v1:
time: 186 us; the launch traced here: 183 us
  Pallas kernels  64.1 us (34%)
  waiting for transfers between devices  28.6 us (15%)
  starting transfers between devices  28.5 us (15%)
  blocking collectives  27.2 us (15%)
  local copies, waits for them, and re-layouts  17.7 us (10%)
  between operations  14.4 us (8%)
  other arithmetic  2.3 us (1%)
    all_to_all x2, waiting for transfers between devices, exchange(): return lax.all_to_all(x, CHIP_AXES, split_axis=0, concat_axis=0, tiled=True)  27.3 us
    pallas_call x1, Pallas kernels, shards(): call(trailing_kernel, 'trailing', (f32(HALF, HALF), f32(HALF, HALF)), [SM...  25.2 us
    all_to_all x2, starting transfers between devices, exchange(): return lax.all_to_all(x, CHIP_AXES, split_axis=0, concat_axis=0, tiled=True)  21.1 us
    pallas_call x1, Pallas kernels, shards(): call(leading_kernel, 'leading', (f32(HALF, HALF), f32(4, BLK, BLK)), [SME...  20.7 us
    unnamed x37, local copies, waits for them, and re-layouts  16.7 us
    all_to_all x1, blocking collectives, shards(): amp = lax.all_to_all(amp, 'freq', split_axis=0, concat_axis=0, tiled=True)  16.2 us
    all_to_all x1, blocking collectives, exchange(): return lax.all_to_all(x, CHIP_AXES, split_axis=0, concat_axis=0, tiled=True)  11 us
    ppermute x3, starting transfers between devices, swap(): return lax.ppermute(x, 'core', [(0, 1), (1, 0)])  7.46 us
  transfers between devices with their start and end apart: 6, of which 3 were waited for; matrix products, arithmetic and copies ran while one was open for 3% of the time, Pallas kernels for 30%

profile of v1, /device:TPU:1, one launch (start us, length us, event | category | flops | bytes accessed | tf_op | source)
XLA Modules:
  0.0 182.8 jit_solution(11117016579068519873)
XLA Ops:
  6.6 1.5 copy-done.5
  8.1 4.0 %schur.1 = (f32[16,144,128]{2,1,0:T(8,128)S(1)}, f32[16,144,128]{2,1,0:T(8,128)S(1)}) custom-call(s32[2]{0:T(128)S(1)} %pad_add_fusion.2.where_ref, bf16[832,1024]{1,0:T(8,128)(2,1)S(1)} %bitcast.27), custom_call_target="tpu_custom_call" | custom-call | flops 1000000000 | bytes 4194304 | tf_op jit(solution)/shard_map/schur/schur/pallas_call | solution.py:387
  12.1 3.3 %collective-permute-start = (f32[16,144,128]{2,1,0:T(8,128)S(1)}, f32[16,144,128]{2,1,0:T(8,128)S(1)}, u32[]{:S(2)}, u32[]{:S(2)}) collective-permute-start(f32[16,144,128]{2,1,0:T(8,128)S(1)} %get-tuple-element.16), channel_id=1, source_target_pairs={{0,1},{1,0},{2,3},{3,2},{4,5},{5,4},{6,7},{7,6},{8,9},{9,8},{10,11... | collective-permute-start | bytes 3538952 | tf_op jit(solution)/shard_map/schur/ppermute | solution.py:375
  15.4 5.1 %prior.1 = f32[1024,1024]{1,0:T(8,128)S(1)} custom-call(bf16[832,1024]{1,0:T(8,128)(2,1)S(1)} %bitcast.28, s32[832,512]{1,0:T(8,128)S(1)} %bitcast.29), custom_call_target="tpu_custom_call" | custom-call | flops 2000000000 | bytes 8388608 | tf_op jit(solution)/shard_map/prior/prior/pallas_call | solution.py:392
  20.5 1.9 %copy-done = f32[1024,1024]{1,0:T(8,128)} copy-done((f32[1024,1024]{1,0:T(8,128)}, f32[1024,1024]{1,0:T(8,128)S(1)}, u32[]{:S(2)}) %copy-start) | copy-done | bytes 4194328
  23.2 1.1 add.219
  24.3 5.2 %all-to-all-start = ((f32[16,144,128]{2,1,0:T(8,128)}), f32[16,144,128]{2,1,0:T(8,128)S(1)}, u32[]{:S(2)}, u32[]{:S(2)}) async-start(f32[16,144,128]{2,1,0:T(8,128)} %add.219), calls=%async_computation | async-start | bytes 2359296 | tf_op jit(solution)/shard_map/reduce/all_to_all | solution.py:371
  30.1 17.9 %all-to-all-done = f32[16,144,128]{2,1,0:T(8,128)S(1)} async-done(((f32[16,144,128]{2,1,0:T(8,128)}), f32[16,144,128]{2,1,0:T(8,128)S(1)}, u32[]{:S(2)}, u32[]{:S(2)}) %all-to-all-start) | async-done | bytes 1179680 | tf_op jit(solution)/shard_map/reduce/all_to_all | solution.py:371
  48.5 11.0 %all_to_all.20.own_ref = f32[16,40,128]{2,1,0:T(8,128)S(1)} all-to-all(f32[16,40,128]{2,1,0:T(8,128)S(1)} %broadcast_in_dim.301), channel_id=1, replica_groups=mesh['freq'=8,'row'=4,'y'=4,'core'=2] {'row','y'}, dimensions={0} | all-to-all | bytes 655360 | tf_op jit(solution)/shard_map/gather_first/all_to_all | solution.py:371
  59.5 2.9 %collective-permute-start.1 = (f32[16,40,128]{2,1,0:T(8,128)S(1)}, f32[16,40,128]{2,1,0:T(8,128)S(1)}, u32[]{:S(2)}, u32[]{:S(2)}) collective-permute-start(f32[16,40,128]{2,1,0:T(8,128)S(1)} %all_to_all.20.own_ref), channel_id=1, source_target_pairs={{0,1},{1,0},{2,3},{3,2},{4,5},{5,4},{6,7},{7,6},{8,9},{9,8},{10,11... | collective-permute-start | bytes 983048 | tf_op jit(solution)/shard_map/gather_first/ppermute | solution.py:375
  62.5 1.3 collective-permute-done.1.other_ref
  63.7 0.8 copy-done.14
  64.5 1.0 broadcast_in_dim.302
  65.4 15.9 %all-to-all-start.2 = ((f32[16,104,128]{2,1,0:T(8,128)}), f32[16,104,128]{2,1,0:T(8,128)}, u32[]{:S(2)}, u32[]{:S(2)}) async-start(f32[16,104,128]{2,1,0:T(8,128)} %broadcast_in_dim.302), calls=%async_computation.2 | async-start | bytes 1703936 | tf_op jit(solution)/shard_map/gather_second/all_to_all | solution.py:371
  81.3 1.9 %copy.9 = s32[1,1024,512]{1,2,0:T(8,128)S(1)} copy(s32[1,1024,512]{2,1,0:T(8,128)} %param.9) | data formatting | bytes 4194304 | tf_op args[2]
  83.3 3.4 %window_waves.1 = (bf16[1024,1024]{1,0:T(8,128)(2,1)S(1)}, bf16[1024,1024]{1,0:T(8,128)(2,1)S(1)}) custom-call(s32[512,1024]{1,0:T(8,128)S(1)} %bitcast.26), custom_call_target="tpu_custom_call" | custom-call | flops 1000000000 | bytes 6291456 | tf_op jit(solution)/shard_map/reduce/window_waves/pallas_call | solution.py:404
  86.7 1.3 copy-done.1
  88.0 1.3 copy-done.3
  89.4 9.4 %all-to-all-done.2.own_ref = f32[16,104,128]{2,1,0:T(8,128)} async-done(((f32[16,104,128]{2,1,0:T(8,128)}), f32[16,104,128]{2,1,0:T(8,128)}, u32[]{:S(2)}, u32[]{:S(2)}) %all-to-all-start.2) | async-done | bytes 852000 | tf_op jit(solution)/shard_map/gather_second/all_to_all | solution.py:371
  98.8 1.2 collective-permute-start.2
  100.0 1.0 copy-done.15
  101.0 20.7 %leading.1 = (f32[512,512]{1,0:T(8,128)S(1)}, f32[4,128,128]{2,1,0:T(8,128)S(1)}) custom-call(s32[2]{0:T(128)S(1)} %pad_add_fusion.2.where_ref, f32[16,40,128]{2,1,0:T(8,128)S(1)} %all_to_all.20.own_ref, f32[16,40,128]{2,1,0:T(8,128)S(1)} %copy-done.15), custom_call_target="tpu_custom_call" | custom-call | flops 20000000000 | bytes 2097152 | tf_op jit(solution)/shard_map/leading/leading/pallas_call | solution.py:423
  121.7 25.2 %trailing.1 = (f32[512,512]{1,0:T(8,128)S(1)}, f32[512,512]{1,0:T(8,128)S(1)}) custom-call(s32[2]{0:T(128)S(1)} %pad_add_fusion.2.where_ref, f32[16,104,128]{2,1,0:T(8,128)} %all-to-all-done.2.own_ref, f32[16,104,128]{2,1,0:T(8,128)S(1)} %collective-permute-done.2.other_ref, f32[512,512]{1,0:T(8,128)S(1)} %get-tuple-element.18.upper_ref, ...), custom_call_target="tpu_custom_call" | custom-call | flops 24999999488 | bytes 4194304 | tf_op jit(solution)/shard_map/trailing/trailing/pallas_call | solution.py:434
  146.9 1.0 copy-done.8
  147.9 1.1 copy-done.10
  148.9 1.6 copy-done.4
  150.5 1.2 copy-done.9
  151.8 1.2 copy-done.11
  153.0 0.9 copy-done.12
  153.9 2.5 %amplitude.1 = f32[8,32,128]{2,1,0:T(8,128)S(1)} custom-call(s32[2]{0:T(128)S(1)} %pad_add_fusion.2.where_ref, f32[512,512]{1,0:T(8,128)S(1)} %get-tuple-element.18.upper_ref, f32[512,512]{1,0:T(8,128)S(1)} %copy-done.9, f32[512,512]{1,0:T(8,128)S(1)} %copy-done.11, bf16[1024,1024]{1,0:T(8,128)(2,1)S(1)} %copy-done.2, bf16[1024,1024]{1,0:T(8,128)(2,1)S(1)} %copy-done.4, ...), custom_call_target="tpu_custom_call" | custom-call | flops 1000000000 | bytes 8388608 | tf_op jit(solution)/shard_map/amplitude/amplitude/pallas_call | solution.py:444
  156.4 16.2 %all_to_all.21.amp_ref = f32[8,32,128]{2,1,0:T(8,128)S(1)} all-to-all(f32[8,32,128]{2,1,0:T(8,128)S(1)} %amplitude.1), channel_id=1, replica_groups=mesh['freq'=8,'row'=4,'y'=4,'core'=2] {'freq'}, dimensions={0} | all-to-all | bytes 262144 | tf_op jit(solution)/shard_map/amplitude/all_to_all | solution.py:452
  172.7 3.2 %synthesis.1 = f32[64,32,256]{2,1,0:T(8,128)} custom-call(f32[8,32,128]{2,1,0:T(8,128)S(1)} %all_to_all.21.amp_ref, f32[16,256]{1,0:T(8,128)S(1)} %copy-done.13), custom_call_target="tpu_custom_call" | custom-call | flops 100000000 | bytes 2097152 | tf_op jit(solution)/shard_map/synthesis/synthesis/pallas_call | solution.py:454
  (44 shorter events, 1.3 us)
Async XLA Ops:
  6.5 142.4 %reduce-scatter.2.cloned.1.call-start = ((), (), s32[]{:S(2)}) async-start(), calls=%async_computation.5 | async-start | bytes 4325376 | tf_op jit(solution)/shard_map/prior/reduce_scatter | solution.py:401
  6.6 1.5 copy-start.5
  8.1 7.3 %copy-start.6 = (bf16[1,832,1024]{2,1,0:T(8,128)(2,1)S(1)}, bf16[1,832,1024]{2,1,0:T(8,128)(2,1)}, u32[]{:S(2)}) copy-start(bf16[1,832,1024]{2,1,0:T(8,128)(2,1)} %param.7) | copy-start | bytes 5111812
  8.1 7.3 %copy-start.7 = (s32[1,832,512]{2,1,0:T(8,128)S(1)}, s32[1,832,512]{2,1,0:T(8,128)}, u32[]{:S(2)}) copy-start(s32[1,832,512]{2,1,0:T(8,128)} %param.8) | copy-start | bytes 5111812
  12.1 11.1 %collective-permute-start = (f32[16,144,128]{2,1,0:T(8,128)S(1)}, f32[16,144,128]{2,1,0:T(8,128)S(1)}, u32[]{:S(2)}, u32[]{:S(2)}) collective-permute-start(f32[16,144,128]{2,1,0:T(8,128)S(1)} %get-tuple-element.16), channel_id=1, source_target_pairs={{0,1},{1,0},{2,3},{3,2},{4,5},{5,4},{6,7},{7,6},{8,9},{9,8},{10,11... | collective-permute-start | bytes 3538952 | tf_op jit(solution)/shard_map/schur/ppermute | solution.py:375
  20.5 1.9 %copy-start = (f32[1024,1024]{1,0:T(8,128)}, f32[1024,1024]{1,0:T(8,128)S(1)}, u32[]{:S(2)}) copy-start(f32[1024,1024]{1,0:T(8,128)S(1)} %prior.1) | copy-start | bytes 12582916
  24.3 5.4 %copy-start.16 = (f32[1,1024]{1,0:T(1,128)S(1)}, f32[1,1024]{1,0:T(1,128)}, u32[]{:S(2)}) copy-start(f32[1,1024]{1,0:T(1,128)} %param.10) | copy-start | bytes 12292
  24.3 5.4 %copy-start.17 = (f32[1,1024]{1,0:T(1,128)S(1)}, f32[1,1024]{1,0:T(1,128)}, u32[]{:S(2)}) copy-start(f32[1,1024]{1,0:T(1,128)} %param.11) | copy-start | bytes 12292
  24.3 23.8 %all-to-all-start = ((f32[16,144,128]{2,1,0:T(8,128)}), f32[16,144,128]{2,1,0:T(8,128)S(1)}, u32[]{:S(2)}, u32[]{:S(2)}) async-start(f32[16,144,128]{2,1,0:T(8,128)} %add.219), calls=%async_computation | async-start | bytes 2359296 | tf_op jit(solution)/shard_map/reduce/all_to_all | solution.py:371
  59.5 4.2 %collective-permute-start.1 = (f32[16,40,128]{2,1,0:T(8,128)S(1)}, f32[16,40,128]{2,1,0:T(8,128)S(1)}, u32[]{:S(2)}, u32[]{:S(2)}) collective-permute-start(f32[16,40,128]{2,1,0:T(8,128)S(1)} %all_to_all.20.own_ref), channel_id=1, source_target_pairs={{0,1},{1,0},{2,3},{3,2},{4,5},{5,4},{6,7},{7,6},{8,9},{9,8},{10,11... | collective-permute-start | bytes 983048 | tf_op jit(solution)/shard_map/gather_first/ppermute | solution.py:375
  63.7 0.8 copy-start.14
  65.4 33.3 %all-to-all-start.2 = ((f32[16,104,128]{2,1,0:T(8,128)}), f32[16,104,128]{2,1,0:T(8,128)}, u32[]{:S(2)}, u32[]{:S(2)}) async-start(f32[16,104,128]{2,1,0:T(8,128)} %broadcast_in_dim.302), calls=%async_computation.2 | async-start | bytes 1703936 | tf_op jit(solution)/shard_map/gather_second/all_to_all | solution.py:371
  86.7 1.3 copy-start.1
  88.0 1.3 copy-start.3
  98.8 22.9 %collective-permute-start.2 = (f32[16,104,128]{2,1,0:T(8,128)}, f32[16,104,128]{2,1,0:T(8,128)S(1)}, u32[]{:S(2)}, u32[]{:S(2)}) collective-permute-start(f32[16,104,128]{2,1,0:T(8,128)} %all-to-all-done.2.own_ref), channel_id=1, source_target_pairs={{0,1},{1,0},{2,3},{3,2},{4,5},{5,4},{6,7},{7,6},{8,9},{9,8},{10,11... | collective-permute-start | bytes 2555912 | tf_op jit(solution)/shard_map/trailing/ppermute | solution.py:375
  100.0 1.0 copy-start.15
  121.7 27.3 %copy-start.2 = (bf16[1024,1024]{1,0:T(8,128)(2,1)S(1)}, bf16[1024,1024]{1,0:T(8,128)(2,1)}, u32[]{:S(2)}) copy-start(bf16[1024,1024]{1,0:T(8,128)(2,1)} %copy-done.1) | copy-start | bytes 6291460
  146.9 1.0 copy-start.8
  147.9 1.1 copy-start.10
  148.9 1.6 copy-start.4
  150.5 1.2 copy-start.9
  151.8 1.2 copy-start.11
  153.0 0.9 copy-start.12
  153.9 18.8 %copy-start.13 = (f32[16,256]{1,0:T(8,128)S(1)}, f32[16,256]{1,0:T(8,128)}, u32[]{:S(2)}) copy-start(f32[16,256]{1,0:T(8,128)} %constant.196.clone.table_ref) | copy-start | bytes 49156
Sparse Core Ops, SparseCore 0:
  22.6 95.2 reduce-scatter.1
